TPU v7x, 32 devices: a whole 2x2x4 slice. The times are simulated.
32 devices in a mesh: grp: 4 (over y, core), dev: 8 (over z, x).
Axes of the slice: x: 2, y: 2, z: 4, core: 2. Of those that a mesh axis runs over, the one named last changes fastest.
Arguments:
- basis_old: float32 [128, 524288], P(None, ('grp', 'dev')), as said below
- values_old: float32 [128], replicated, may hold values from 1 to 4
- snapshots: float32 [2, 64, 524288], P(None, None, ('grp', 'dev'))
- wet_counts: int32 [32], P(('grp', 'dev')), may hold values from 1 to 128, as said below
Outputs:
- basis_new: float32 [128, 524288], P(None, ('grp', 'dev'))
- values_new: float32 [128], replicated
Inputs may be any that keep to these rules, and one draw needn't show every extreme that they name: `wet_counts`: every device has at least one wet block, and some device has all 128 blocks wet. basis_old is zero on every cell that wet_mask marks dry.
All inputs are finite; a program needn't handle non-finite values.
Results may differ from a plain program's by a relative error of at most 0.0003.
Values sent between devices are 32-bit elements; how exact they have to be, the bound alone decides.
A program may use at most 128 MiB of HBM per device.

v0:
```python
import functools

import jax
import jax.numpy as jnp
from jax import lax
from jax.experimental import pallas as pl
from jax.experimental.pallas import tpu as pltpu
from jax.sharding import PartitionSpec as P

BLOCK = 128
SWEEPS = 3
PANEL = 32
SUB = 8
TILE = 2048
MESH = pl.DeviceIdType.MESH
F32 = jnp.float32
BF16 = jnp.bfloat16


def dot_half(left_op, right_op, dims):
    return lax.dot_general(left_op, right_op, (dims, ((), ())), preferred_element_type=F32)


def split_two(x):
    high = x.astype(BF16)
    return high, (x - high.astype(F32)).astype(BF16)


def split_three(x):
    high = x.astype(BF16)
    rest = x - high.astype(F32)
    mid = rest.astype(BF16)
    return high, mid, (rest - mid.astype(F32)).astype(BF16)


def dot_full(left_op, right_op, dims):
    left_axis = 1 - dims[0][0]
    rows = left_op.shape[left_axis]
    left_terms, right_terms = split_three(left_op), split_three(right_op)
    total = None
    for place in (2, 1, 0):
        used = 3 - place
        stacked = jnp.concatenate(left_terms[:used], left_axis)
        product = dot_half(stacked, right_terms[place], dims)
        part = product[:rows, :]
        if used > 1:
            small = product[rows : 2 * rows, :]
            if used > 2:
                small = small + product[2 * rows :, :]
            part = part + small
        total = part if total is None else part + total
    return total


def nn(left_op, right_op):
    return dot_full(left_op, right_op, ((1,), (0,)))


def nt(left_op, right_op):
    return dot_full(left_op, right_op, ((1,), (1,)))


def tn(left_op, right_op):
    return dot_full(left_op, right_op, ((0,), (0,)))


def self_nt(op):
    rows = op.shape[0]
    high, mid, low = split_three(op)
    dims = ((1,), (1,))
    product = dot_half(jnp.concatenate([high, mid, low], 0), high, dims)
    cross = product[rows : 2 * rows, :] + product[2 * rows :, :]
    return product[:rows, :] + (cross + cross.T + dot_half(mid, mid, dims))


def stack_copies(basis_hbm, snaps_hbm, stack, basis_sem, snaps_sem, i):
    rank, updates, batch = basis_hbm.shape[0], snaps_hbm.shape[0], snaps_hbm.shape[1]
    tile = stack.shape[2]
    spot = pl.ds(pl.multiple_of(i * tile, tile), tile)
    return [
        pltpu.make_async_copy(basis_hbm.at[:, spot], stack.at[i, pl.ds(0, rank)], basis_sem.at[i])
    ] + [
        pltpu.make_async_copy(
            snaps_hbm.at[t, :, spot],
            stack.at[i, pl.ds(rank + t * batch, batch)],
            snaps_sem.at[t, i],
        )
        for t in range(updates)
    ]


def masked_parts(counts_ref, stack, rank, i):
    snaps = stack[i, rank:, :]
    cell = i * stack.shape[2] + lax.broadcasted_iota(jnp.int32, snaps.shape, 1)
    snaps = jnp.where(cell < counts_ref[0] * BLOCK, snaps, 0.0)
    return split_two(jnp.concatenate([stack[i, :rank, :], snaps], 0))


def pack_gram(total, count, rank, out_ref):
    row = 0
    for i in range(total.shape[0] // rank):
        for j in range(i + 1):
            block = total[i * rank : (i + 1) * rank, j * rank : (j + 1) * rank]
            if i == 0:
                spot = (lax.broadcasted_iota(jnp.int32, block.shape, 0) == 0) & (
                    lax.broadcasted_iota(jnp.int32, block.shape, 1) == rank - 1
                )
                block = jnp.where(spot, count, block)
            out_ref[row : row + rank, :] = block
            row += rank
    if row < out_ref.shape[0]:
        out_ref[row:, :] = jnp.zeros((out_ref.shape[0] - row, out_ref.shape[1]), F32)


def gram_kernel(
    groups, near, far, counts_ref, basis_hbm, snaps_hbm, out_ref,
    stack, main, cross, in_ref, near_buf, far_buf, all_buf, basis_sem, snaps_sem,
    near_send, near_recv, far_send, far_recv, back_send, back_recv,
):
    grp, dev = lax.axis_index("grp"), lax.axis_index("dev")
    level, across = dev // near, lax.rem(dev, near)
    members = groups * near
    me = grp * near + across
    chunk = in_ref.shape[0] // members

    def member(offset):
        rank = lax.rem(me + offset, members)
        return rank, (rank // near, level * near + lax.rem(rank, near))

    def along(offset):
        return (grp, lax.rem(level + offset, far) * near + across)

    barrier = pltpu.get_barrier_semaphore()
    for offset in range(1, members):
        pl.semaphore_signal(barrier, inc=1, device_id=member(offset)[1], device_id_type=MESH)
    for offset in range(1, far):
        pl.semaphore_signal(barrier, inc=1, device_id=along(offset), device_id_type=MESH)

    tiles = stack.shape[0]
    rank_width = basis_hbm.shape[0]

    def fetch(i, carry):
        for copy in stack_copies(basis_hbm, snaps_hbm, stack, basis_sem, snaps_sem, i):
            copy.start()
        return carry

    lax.fori_loop(0, tiles, fetch, 0)
    main[...] = jnp.zeros_like(main)
    cross[...] = jnp.zeros_like(cross)

    def accumulate(i, carry):
        for copy in stack_copies(basis_hbm, snaps_hbm, stack, basis_sem, snaps_sem, i):
            copy.wait()
        high, low = masked_parts(counts_ref, stack, rank_width, i)
        dims = ((1,), (1,))
        main[...] += dot_half(high, high, dims) + dot_half(low, low, dims)
        cross[...] += dot_half(high, low, dims)
        return carry

    lax.fori_loop(0, tiles, accumulate, 0)
    total = main[...] + cross[...] + cross[...].T
    pack_gram(total, counts_ref[0].astype(F32), rank_width, in_ref)
    pl.semaphore_wait(barrier, members - 1 + far - 1)

    copies = []
    for offset in range(1, members):
        rank, where = member(offset)
        copies.append(
            pltpu.make_async_remote_copy(
                src_ref=in_ref.at[pl.ds(pl.multiple_of(rank * chunk, SUB), chunk)],
                dst_ref=near_buf.at[offset],
                send_sem=near_send.at[offset],
                recv_sem=near_recv.at[offset],
                device_id=where,
                device_id_type=MESH,
            )
        )
        copies[-1].start()
    mine = pl.ds(pl.multiple_of(me * chunk, SUB), chunk)
    total = in_ref[mine, :]
    for offset, copy in enumerate(copies, 1):
        copy.wait_recv()
        total = total + near_buf[offset]
    far_buf[level] = total
    sends = copies

    copies = []
    for offset in range(1, far):
        copies.append(
            pltpu.make_async_remote_copy(
                src_ref=far_buf.at[level],
                dst_ref=far_buf.at[level],
                send_sem=far_send.at[offset],
                recv_sem=far_recv.at[offset],
                device_id=along(offset),
                device_id_type=MESH,
            )
        )
        copies[-1].start()
    for copy in copies:
        copy.wait_recv()
    sends = sends + copies
    total = far_buf[0]
    for other in range(1, far):
        total = total + far_buf[other]
    all_buf[mine, :] = total

    copies = []
    for offset in range(1, members):
        copies.append(
            pltpu.make_async_remote_copy(
                src_ref=all_buf.at[mine],
                dst_ref=all_buf.at[mine],
                send_sem=back_send.at[offset],
                recv_sem=back_recv.at[offset],
                device_id=member(offset)[1],
                device_id_type=MESH,
            )
        )
        copies[-1].start()
    for copy in copies:
        copy.wait_recv()
    for copy in sends + copies:
        copy.wait_send()
    out_ref[...] = all_buf[...]


def eliminate(panel, start):
    diagonal, arrays = panel
    halves = PANEL // SUB
    lanes = diagonal.shape[1]
    cols = [
        {
            h: jnp.broadcast_to(diagonal[h * SUB : (h + 1) * SUB, start + j : start + j + 1], (SUB, lanes))
            for h in range(j // SUB, halves)
        }
        for j in range(PANEL)
    ]
    work = [[a[h * SUB : (h + 1) * SUB, :] for h in range(halves)] for a in arrays]
    row = lax.broadcasted_iota(jnp.int32, (SUB, lanes), 0)
    pivots = [jnp.ones((SUB, lanes), F32) for _ in range(halves)]
    pivot = jnp.broadcast_to(cols[0][0][0:1, :], (SUB, lanes))
    for j in range(PANEL):
        half, sub = j // SUB, j % SUB
        pivots[half] = jnp.where(row == sub, pivot, pivots[half])
        guess = pl.reciprocal(pivot, approx=True)
        fix = 2.0 - pivot * guess
        if j + 1 < PANEL:
            ahead, spot = (j + 1) // SUB, (j + 1) % SUB
            lead = jnp.broadcast_to(cols[j][ahead][spot : spot + 1, :], (SUB, lanes))
            pivot = jnp.broadcast_to(cols[j + 1][ahead][spot : spot + 1, :], (SUB, lanes))
            pivot = pivot - ((lead * guess) * lead) * fix
        scaled = {h: (cols[j][h] * guess) * fix for h in range(half, halves)}
        for k in range(j + 1, PANEL):
            lead = jnp.broadcast_to(cols[j][k // SUB][k % SUB : k % SUB + 1, :], (SUB, lanes))
            for h in range(k // SUB, halves):
                cols[k][h] = cols[k][h] - scaled[h] * lead
        below = {**scaled, half: jnp.where(row > sub, scaled[half], 0.0)}
        for target in work:
            lead = jnp.broadcast_to(target[half][sub : sub + 1, :], (SUB, lanes))
            for h in range(half, halves):
                target[h] = target[h] - below[h] * lead
    out = []
    scales = []
    for h in range(halves):
        guess = lax.rsqrt(pivots[h])
        scales.append(guess * (1.5 - 0.5 * pivots[h] * guess * guess))
    for target in work:
        out.append(jnp.concatenate([target[h] * scales[h] for h in range(halves)], 0))
    return out


def outer_rows(rows, first):
    high, mid, low = split_three(rows)
    left = jnp.concatenate([high, high, mid, high, mid, low], 0)
    right = jnp.concatenate([high, mid, high, low, mid, high], 0)
    return dot_half(left, right, ((0,), (0,)))[first:, :]


def lower_inverse(ref, size):
    for start in range(0, size, PANEL):
        stop = start + PANEL
        rows = ref[start:stop, :]
        lane = lax.broadcasted_iota(jnp.int32, rows.shape, 1)
        sub = lax.broadcasted_iota(jnp.int32, rows.shape, 0)
        inside = (lane >= start) & (lane < stop)
        eye = (lane == sub + start).astype(F32)
        (rows,) = eliminate((rows, [jnp.where(inside, eye, rows)]), start)
        ref[start:stop, :] = rows
        if stop < size:
            rest = ref[stop:, :]
            lane = lax.broadcasted_iota(jnp.int32, rest.shape, 1)
            rest = jnp.where((lane >= start) & (lane < stop), 0.0, rest)
            masked = rows
            ref[stop:, :] = rest - outer_rows(masked, stop)[: size - stop, :]


def factor_and_inverse(ref, size):
    for start in range(0, size, PANEL):
        stop = start + PANEL
        rows = ref[start:stop, :]
        (rows,) = eliminate((rows, [rows]), start)
        ref[start:stop, :] = rows
        if stop < size:
            ref[stop:, :] = ref[stop:, :] - outer_rows(rows, stop)[: size - stop, :]


def core_kernel(
    batch, updates, counts_ref, sum_ref, values_ref, basis_hbm, snaps_hbm, out_hbm, new_values_ref,
    gram, core, square, frame, big, small, coeff_ref, stack, result, basis_sem, snaps_sem, out_sem,
):
    rank = values_ref.shape[1]
    tiles, _, tile = stack.shape

    def tile_copies(i):
        return stack_copies(basis_hbm, snaps_hbm, stack, basis_sem, snaps_sem, i)

    def out_copy(i):
        spot = pl.ds(pl.multiple_of(i * tile, tile), tile)
        return pltpu.make_async_copy(result.at[i], out_hbm.at[:, spot], out_sem.at[i])

    def fetch(i, carry):
        for copy in tile_copies(i):
            copy.start()
        return carry

    lax.fori_loop(0, tiles, fetch, 0)
    width = gram.shape[0]
    rows = lax.broadcasted_iota(jnp.int32, (rank, rank), 0)
    lanes = lax.broadcasted_iota(jnp.int32, (rank, rank), 1)
    eye = rows == lanes
    count = sum_ref[0:1, rank - 1 : rank]
    wet_total = count * BLOCK
    parts = width // rank
    row = 0
    for i in range(parts):
        for j in range(i + 1):
            block = sum_ref[row : row + rank, :]
            row += rank
            if i == 0:
                block = jnp.where((rows == 0) & (lanes == rank - 1), block.T, block)
            gram[i * rank : (i + 1) * rank, j * rank : (j + 1) * rank] = block
            if i != j:
                gram[j * rank : (j + 1) * rank, i * rank : (i + 1) * rank] = block.T

    wide_rows = lax.broadcasted_iota(jnp.int32, (rank, width), 0)
    wide_lanes = lax.broadcasted_iota(jnp.int32, (rank, width), 1)
    start_frame = (wide_rows == wide_lanes).astype(F32)
    coeff_ref[...] = start_frame
    core[...] = jnp.zeros_like(core)
    diag = jnp.where(eye, values_ref[...], 0.0)

    batch_rows = lax.broadcasted_iota(jnp.int32, (batch, width), 0)
    batch_lanes = lax.broadcasted_iota(jnp.int32, (batch, width), 1)
    small_rows = lax.broadcasted_iota(jnp.int32, (batch, batch), 0)
    small_lanes = lax.broadcasted_iota(jnp.int32, (batch, batch), 1)

    for index in range(updates):
        coeff = coeff_ref[...]
        first = rank + index * batch
        projected = gram[:rank, :] if index == 0 else nn(coeff, gram[...])
        project = projected[:, first : first + batch] / wet_total
        picker = (batch_lanes == first + batch_rows).astype(F32)
        if index == 0:
            remain = picker - jnp.concatenate(
                [project.T, jnp.zeros((batch, width - rank), F32)], 1
            )
        else:
            remain = picker - tn(project, coeff)
        small[:, :batch] = nt(nn(remain, gram[...]), remain) / wet_total
        small[:, batch:] = (small_rows == small_lanes).astype(F32)
        factor_and_inverse(small, batch)
        factor_t = jnp.where(small_lanes >= small_rows, small[:, :batch], 0.0)
        fresh = nn(small[:, batch:], remain)
        core[:rank, :rank] = diag
        core[:rank, rank : rank + batch] = project
        core[rank : rank + batch, rank : rank + batch] = factor_t
        square[...] = self_nt(core[...])

        def sweep(step, carry):
            @pl.when(step == 0)
            def _():
                frame[...] = square[:rank, :]

            @pl.when(step > 0)
            def _():
                frame[...] = nn(frame[...], square[...])

            grown = frame[...]
            big[...] = self_nt(grown)
            lower_inverse(big, rank)
            inverse = jnp.where(lanes <= rows, big[...], 0.0)
            frame[...] = nn(inverse, grown)
            return carry

        lax.fori_loop(0, SWEEPS, sweep, 0)
        frame_now = frame[...]
        rotated = nn(frame_now, core[...])
        lengths = jnp.sqrt(jnp.sum(rotated * rotated, axis=1, keepdims=True))
        diag = jnp.where(eye, lengths, 0.0)
        if index == 0:
            carried = jnp.concatenate(
                [frame_now[:, :rank], jnp.zeros((rank, width - rank), F32)], 1
            )
        else:
            carried = nn(frame_now[:, :rank], coeff)
        coeff_ref[...] = carried + nn(frame_now[:, rank : rank + batch], fresh)
    new_values_ref[...] = jnp.sum(diag, axis=0, keepdims=True)

    coeff_high, coeff_low = split_two(coeff_ref[...])
    coeff_both = jnp.concatenate([coeff_high, coeff_low], 0)
    dims = ((1,), (0,))

    def apply(i, carry):
        for copy in tile_copies(i):
            copy.wait()
        high, low = masked_parts(counts_ref, stack, rank, i)
        both = dot_half(coeff_both, high, dims)
        result[i] = both[:rank, :] + (both[rank:, :] + dot_half(coeff_high, low, dims))
        out_copy(i).start()
        return carry

    lax.fori_loop(0, tiles, apply, 0)

    def drain(i, carry):
        out_copy(i).wait()
        return carry

    lax.fori_loop(0, tiles, drain, 0)


def per_device(groups, devs, basis_old, values_old, snapshots, wet_counts):
    rank, cells = basis_old.shape
    updates, batch = snapshots.shape[0], snapshots.shape[1]
    width = rank + updates * batch
    near = 1
    while (2 * near) * (2 * near) <= devs and devs % (2 * near) == 0:
        near *= 2
    far = devs // near
    members = groups * near
    parts = width // rank
    rows = rank * parts * (parts + 1) // 2
    chunk = -(-rows // (members * SUB)) * SUB
    padded = chunk * members
    tile = min(TILE, cells)

    tiles = cells // tile
    smem = pl.BlockSpec(memory_space=pltpu.SMEM)
    vmem = pl.BlockSpec(memory_space=pltpu.VMEM)
    hbm = pl.BlockSpec(memory_space=pl.ANY)
    summed = pl.pallas_call(
        functools.partial(gram_kernel, groups, near, far),
        out_shape=jax.ShapeDtypeStruct((padded, rank), F32),
        in_specs=[smem, hbm, hbm],
        out_specs=vmem,
        scratch_shapes=[
            pltpu.VMEM((tiles, width, tile), F32),
            pltpu.VMEM((width, width), F32),
            pltpu.VMEM((width, width), F32),
            pltpu.VMEM((padded, rank), F32),
            pltpu.VMEM((members, chunk, rank), F32),
            pltpu.VMEM((far, chunk, rank), F32),
            pltpu.VMEM((padded, rank), F32),
            pltpu.SemaphoreType.DMA((tiles,)),
            pltpu.SemaphoreType.DMA((updates, tiles)),
            pltpu.SemaphoreType.DMA((members,)),
            pltpu.SemaphoreType.DMA((members,)),
            pltpu.SemaphoreType.DMA((far,)),
            pltpu.SemaphoreType.DMA((far,)),
            pltpu.SemaphoreType.DMA((members,)),
            pltpu.SemaphoreType.DMA((members,)),
        ],
        compiler_params=pltpu.CompilerParams(
            collective_id=0, has_side_effects=True, vmem_limit_bytes=52 << 20
        ),
    )(wet_counts, basis_old, snapshots)

    basis_new, values = pl.pallas_call(
        functools.partial(core_kernel, batch, updates),
        out_shape=(
            jax.ShapeDtypeStruct((rank, cells), F32),
            jax.ShapeDtypeStruct((1, rank), F32),
        ),
        in_specs=[smem, vmem, vmem, hbm, hbm],
        out_specs=(hbm, vmem),
        scratch_shapes=[
            pltpu.VMEM((width, width), F32),
            pltpu.VMEM((width, width), F32),
            pltpu.VMEM((width, width), F32),
            pltpu.VMEM((rank, width), F32),
            pltpu.VMEM((rank, rank), F32),
            pltpu.VMEM((batch, 2 * batch), F32),
            pltpu.VMEM((rank, width), F32),
            pltpu.VMEM((tiles, width, tile), F32),
            pltpu.VMEM((tiles, rank, tile), F32),
            pltpu.SemaphoreType.DMA((tiles,)),
            pltpu.SemaphoreType.DMA((updates, tiles)),
            pltpu.SemaphoreType.DMA((tiles,)),
        ],
        compiler_params=pltpu.CompilerParams(vmem_limit_bytes=52 << 20),
    )(wet_counts, summed, values_old.reshape(1, rank), basis_old, snapshots)
    return basis_new, values.reshape(rank)


def solution(mesh):
    return jax.shard_map(
        functools.partial(per_device, mesh.shape["grp"], mesh.shape["dev"]),
        mesh=mesh,
        in_specs=(P(None, ("grp", "dev")), P(), P(None, None, ("grp", "dev")), P(("grp", "dev"))),
        out_specs=(P(None, ("grp", "dev")), P()),
        check_vma=False,
    )
```

profile of v0, /device:TPU:0, one launch (start us, length us, event | category | flops | bytes accessed | tf_op | source)
XLA Modules:
  0.0 63.3 jit_solution(3326633742867284877)
XLA Ops:
  1.3 0.0 copy-start
  1.3 25.9 %shard_map.59.sum_ref = f32[384,128]{1,0:T(8,128)S(1)} custom-call(s32[1]{0:T(128)S(6)} %copy.6.counts_ref, f32[128,16384]{1,0:T(8,128)} %basis_hbm.3, f32[2,64,16384]{2,1,0:T(8,128)} %snaps_hbm.3), custom_call_target="tpu_custom_call" | custom-call | tf_op jit(solution)/shard_map/pallas_call | solution.py:451
  27.2 0.0 copy-done
  27.2 36.1 %shard_map.60 = (f32[128,16384]{1,0:T(8,128)}, f32[1,128]{1,0:T(1,128)}) custom-call(s32[1]{0:T(128)S(6)} %copy.6.counts_ref, f32[384,128]{1,0:T(8,128)S(1)} %shard_map.59.sum_ref, f32[1,128]{1,0:T(1,128)S(1)} %bitcast.2, f32[128,16384]{1,0:T(8,128)} %basis_hbm.3, f32[2,64,16384]{2,1,0:T(8,128)} %snaps_hbm.3), custom_call_target="tpu_custom_call" | custom-call | tf_op jit(solution)/shard_map/pallas_call | solution.py:478
Async XLA Ops:
  1.3 25.9 %copy-start = (f32[128]{0:T(128)S(1)}, f32[128]{0:T(128)}, u32[]{:S(2)}) copy-start(f32[128]{0:T(128)} %param.5) | copy-start | bytes 1540
where the time goes:
time: 63.5 us; the launch traced here: 63.3 us
  Pallas kernels  62 us (98%)
  between operations  1.3 us (2%)
    pallas_call x1, Pallas kernels, per_device(): pl.pallas_call(functools.partial(core_kernel, batch, updates), out_shape=...  36.1 us
    pallas_call x1, Pallas kernels, per_device(): pl.pallas_call(functools.partial(gram_kernel, groups, near, far), out_sha...  25.9 us

commit v1 on v0

--- a/solution.py
+++ b/solution.py
@@ -9,7 +9,7 @@
 
 BLOCK = 128
 SWEEPS = 3
-PANEL = 32
+PANEL = 16
 SUB = 8
 TILE = 2048
 MESH = pl.DeviceIdType.MESH

time: 63.5 us -> 66.1 us (1.041)
  Pallas kernels: 62 us -> 64.6 us
    pallas_call x1, Pallas kernels: 36.1 us -> 38.8 us  [per_device(): pl.pallas_call(functools.partial(core_kernel, batch, updates), out_shape=...]
where the time goes in v1:
time: 66.1 us; the launch traced here: 66 us
  Pallas kernels  64.6 us (98%)
  between operations  1.3 us (2%)
    pallas_call x1, Pallas kernels, per_device(): pl.pallas_call(functools.partial(core_kernel, batch, updates), out_shape=...  38.8 us
    pallas_call x1, Pallas kernels, per_device(): pl.pallas_call(functools.partial(gram_kernel, groups, near, far), out_sha...  25.9 us

profile of v1, /device:TPU:0, one launch (start us, length us, event | category | flops | bytes accessed | tf_op | source)
XLA Modules:
  0.0 66.0 jit_solution(13145053202223569917)
XLA Ops:
  1.3 0.0 copy-start
  1.3 25.9 %shard_map.59.sum_ref = f32[384,128]{1,0:T(8,128)S(1)} custom-call(s32[1]{0:T(128)S(6)} %copy.6.counts_ref, f32[128,16384]{1,0:T(8,128)} %basis_hbm.3, f32[2,64,16384]{2,1,0:T(8,128)} %snaps_hbm.3), custom_call_target="tpu_custom_call" | custom-call | tf_op jit(solution)/shard_map/pallas_call | solution.py:451
  27.2 0.0 copy-done
  27.2 38.8 %shard_map.60 = (f32[128,16384]{1,0:T(8,128)}, f32[1,128]{1,0:T(1,128)}) custom-call(s32[1]{0:T(128)S(6)} %copy.6.counts_ref, f32[384,128]{1,0:T(8,128)S(1)} %shard_map.59.sum_ref, f32[1,128]{1,0:T(1,128)S(1)} %bitcast.2, f32[128,16384]{1,0:T(8,128)} %basis_hbm.3, f32[2,64,16384]{2,1,0:T(8,128)} %snaps_hbm.3), custom_call_target="tpu_custom_call" | custom-call | tf_op jit(solution)/shard_map/pallas_call | solution.py:478
Async XLA Ops:
  1.3 25.9 %copy-start = (f32[128]{0:T(128)S(1)}, f32[128]{0:T(128)}, u32[]{:S(2)}) copy-start(f32[128]{0:T(128)} %param.5) | copy-start | bytes 1540
